TPU v7x, 32 devices: a whole 2x2x4 slice. The times are simulated.
32 devices in a mesh: grp: 2 (over y), row: 4 (over z), col: 2 (over x), rep: 2 (over core).
Axes of the slice: x: 2, y: 2, z: 4, core: 2. Of those that a mesh axis runs over, the one named last changes fastest.
Arguments:
- integrals: bfloat16 [512, 32, 512], P(None, ('grp', 'col', 'rep'), 'row'), parts along dimension 1, may hold values from -6 to 6
- occupied: bfloat16 [1024, 512], P(('grp', 'row', 'col')), parts along dimension 0, may hold values from -0.25 to 0.25
- virtual: bfloat16 [1024, 512], P(('grp', 'row', 'col')), parts along dimension 0, may hold values from -0.25 to 0.25
- pair_mask: int32 [4, 4], replicated, may hold values from 0 to 1, as said below
- occ_mask: int32 [4, 4], replicated, may hold values from 0 to 1, as said below
- virt_mask: int32 [4, 4], replicated, may hold values from 0 to 1, as said below
- block_sizes: int32 [4], replicated, may hold values from 64 to 128, as said below
Outputs:
- product: bfloat16 [512, 32, 512], P('row', ('grp', 'col', 'rep')), parts along dimension 1
There are 2 independent parts, one for each index of `grp`. A program takes and returns all parts, laid end to end along the dimension named above; an argument that names none is the same for every part. Nothing has to cross between parts.
Inputs may be any that keep to these rules, and one draw needn't show every extreme that they name: `pair_mask`: each column holds between 1 and 2 ones; some column holds exactly 2. `occ_mask`: diagonal blocks are 1. `virt_mask`: diagonal blocks are 1. `block_sizes`: some block holds exactly 128 functions and some other block exactly 64.
All inputs are finite; a program needn't handle non-finite values.
Results may differ from a plain program's by a relative error of at most 0.005.
Values may be sent and summed in bfloat16 or wider, within the bound.
A program may use at most 64 MiB of HBM per device.

v0:
```python
import jax
import jax.numpy as jnp
from jax import lax
from jax.sharding import PartitionSpec as P

BS = 128


def live_vector(block_sizes, block_count):
    within = lax.broadcasted_iota(jnp.int32, (block_count, BS), 1)
    return (within < block_sizes[:, None]).astype(jnp.float32).reshape(-1)


def one_hot(indices, block_count):
    return (indices[:, None] == lax.broadcasted_iota(jnp.int32, (1, block_count), 1)).astype(
        jnp.float32
    )


def density_shard(density, block_mask, active, shard_index):
    shard_rows = density.shape[0]
    first_row = shard_index * shard_rows
    row_ids = first_row + lax.broadcasted_iota(jnp.int32, (shard_rows,), 0)
    block_rows = jnp.dot(
        one_hot(row_ids // BS, block_mask.shape[0]), block_mask.astype(jnp.float32)
    )
    spread = jnp.repeat(block_rows, BS, axis=1)
    row_active = lax.dynamic_slice_in_dim(active, first_row, shard_rows)
    factor = spread * active[None, :] * row_active[:, None]
    return density * factor.astype(jnp.bfloat16)


def per_device(integrals, occupied, virtual, pair_mask, occ_mask, virt_mask, block_sizes):
    total_ao = integrals.shape[0]
    aux_local = integrals.shape[1]
    ao_local = integrals.shape[2]
    block_count = block_sizes.shape[0]
    active = live_vector(block_sizes, block_count)
    shard_index = lax.axis_index(("row", "col"))
    occ_part = density_shard(occupied, occ_mask, active, shard_index)
    virt_part = density_shard(virtual, virt_mask, active, shard_index)
    first_col = lax.axis_index("row") * ao_local
    column_block = (lax.broadcasted_iota(jnp.int32, (block_count,), 0) == first_col // BS).astype(
        jnp.float32
    )
    column_mask = jnp.dot(pair_mask.astype(jnp.float32), column_block)
    mu_factor = jnp.repeat(column_mask, BS) * active
    nu_factor = lax.dynamic_slice_in_dim(active, first_col, ao_local)
    factor = (mu_factor[:, None, None] * nu_factor[None, None, :]).astype(jnp.bfloat16)
    tensor = integrals * factor
    flat_cols = aux_local * ao_local
    operand = tensor.reshape(total_ao, flat_cols)
    halfway = jnp.dot(
        lax.all_gather(occ_part, ("row", "col"), axis=0, tiled=True),
        operand,
        preferred_element_type=jnp.float32,
    ).astype(jnp.bfloat16)
    virt_full = lax.all_gather(virt_part, ("row", "col"), axis=0, tiled=True)
    halfway = halfway.reshape(total_ao, aux_local, ao_local)
    slices = lax.all_to_all(halfway, "row", split_axis=0, concat_axis=2, tiled=True)
    lead_rows = slices.shape[0]
    item_count = slices.shape[1]
    flattened = slices.reshape(lead_rows * item_count, total_ao)
    result = jnp.dot(flattened, virt_full, preferred_element_type=jnp.float32).astype(jnp.bfloat16)
    return result.reshape(lead_rows, item_count, total_ao)


def solution(mesh):
    in_specs = (
        P(None, ("grp", "col", "rep"), "row"),
        P(("grp", "row", "col"), None),
        P(("grp", "row", "col"), None),
        P(),
        P(),
        P(),
        P(),
    )
    out_specs = P("row", ("grp", "col", "rep"), None)
    return jax.shard_map(
        per_device, mesh=mesh, in_specs=in_specs, out_specs=out_specs, check_vma=False
    )
```

profile of v0, /device:TPU:0, one launch (start us, length us, event | category | flops | bytes accessed | tf_op | source)
XLA Modules:
  0.0 81.7 jit_solution(9117349788491685478)
XLA Ops:
  0.0 0.0 copy-start.4
  0.0 0.6 copy-done.4
  0.7 0.1 convert_bitcast_fusion
  0.7 0.0 copy-start.3
  0.7 0.7 copy-done.3
  1.4 0.1 convolution_bitcast_fusion
  1.5 0.1 select_bitcast_fusion
  1.6 0.0 copy-start.5
  1.6 0.1 dynamic_slice.8
  1.7 0.1 dynamic_slice.7
  1.8 0.5 copy-done.5
  2.3 0.0 copy-start.6
  2.3 0.2 fusion.11
  2.5 0.5 copy-done.6
  3.0 0.2 fusion.10
  3.2 0.1 broadcast_in_dim.8
  3.3 0.0 copy-start.1
  3.3 0.0 copy-start.2
  3.3 0.1 broadcast_in_dim.6
  3.5 0.7 copy-done.1
  4.1 0.0 copy-done.2
  4.2 0.0 copy-start
  4.2 0.1 fusion.8
  4.3 33.2 %all_gather.6 = bf16[512,512]{1,0:T(8,128)(2,1)S(1)} all-gather(bf16[64,512]{1,0:T(8,128)(2,1)S(1)} %get-tuple-element.5), channel_id=1, replica_groups=mesh['grp'=2,'row'=4,'col'=2,'rep'=2] {'row','col'}, dimensions={0}, use_global_device_ids=true | all-gather | bytes 589824 | tf_op jit(solution)/shard_map/all_gather | solution.py:54
  37.4 0.1 multiply_convert_fusion
  37.6 0.0 copy-done
  37.6 0.3 broadcast_multiply_fusion
  37.9 0.5 convolution_convert_fusion.1
  38.4 1.1 %copy.17 = bf16[512,4,128]{2,1,0:T(4,128)(2,1)} copy(bf16[512,4,128]{0,2,1:T(8,128)(2,1)S(1)} %bitcast.46) | data formatting | bytes 1048576 | tf_op jit(solution)/shard_map/reshape | solution.py:59
  39.5 3.5 %all-to-all-start = ((bf16[512,4,128]{2,1,0:T(4,128)(2,1)}), bf16[512,4,128]{2,1,0:T(4,128)(2,1)S(1)}, u32[]{:S(2)}, u32[]{:S(2)}) async-start(bf16[512,4,128]{2,1,0:T(4,128)(2,1)} %copy.17), calls=%async_computation | async-start | bytes 1048576 | tf_op jit(solution)/shard_map/all_to_all | solution.py:60
  42.9 36.9 %all_gather.7 = bf16[512,512]{1,0:T(8,128)(2,1)S(1)} all-gather(bf16[64,512]{1,0:T(8,128)(2,1)S(1)} %get-tuple-element.6), channel_id=1, replica_groups=mesh['grp'=2,'row'=4,'col'=2,'rep'=2] {'row','col'}, dimensions={0}, use_global_device_ids=true | all-gather | bytes 589824 | tf_op jit(solution)/shard_map/all_gather | solution.py:58
  79.9 0.0 all-to-all-done
  79.9 0.1 copy.18
  80.0 0.4 copy.19
  80.4 0.4 convolution_convert_fusion
  80.8 0.9 %reshape.113 = bf16[128,4,512]{2,1,0:T(4,128)(2,1)} reshape(bf16[512,512]{1,0:T(8,128)(2,1)S(1)} %convolution_convert_fusion) | data formatting | bytes 1048576 | tf_op jit(solution)/shard_map/reshape | solution.py:65
  (1 shorter events, 0.0 us)
Async XLA Ops:
  0.0 0.7 copy-start.4
  0.7 0.7 copy-start.3
  1.6 0.7 copy-start.5
  2.3 0.7 copy-start.6
  3.3 0.8 %copy-start.1 = (bf16[64,512]{1,0:T(8,128)(2,1)S(1)}, bf16[64,512]{1,0:T(8,128)(2,1)}, u32[]{:S(2)}) copy-start(bf16[64,512]{1,0:T(8,128)(2,1)} %param.8) | copy-start | bytes 196612
  3.3 0.9 %copy-start.2 = (bf16[64,512]{1,0:T(8,128)(2,1)S(1)}, bf16[64,512]{1,0:T(8,128)(2,1)}, u32[]{:S(2)}) copy-start(bf16[64,512]{1,0:T(8,128)(2,1)} %param.9) | copy-start | bytes 196612
  4.2 33.4 %copy-start = (bf16[512,4,128]{2,1,0:T(4,128)(2,1)S(1)}, bf16[512,4,128]{2,1,0:T(4,128)(2,1)}, u32[]{:S(2)}) copy-start(bf16[512,4,128]{2,1,0:T(4,128)(2,1)} %param.7) | copy-start | bytes 1572868
  39.5 40.4 %all-to-all-start = ((bf16[512,4,128]{2,1,0:T(4,128)(2,1)}), bf16[512,4,128]{2,1,0:T(4,128)(2,1)S(1)}, u32[]{:S(2)}, u32[]{:S(2)}) async-start(bf16[512,4,128]{2,1,0:T(4,128)(2,1)} %copy.17), calls=%async_computation | async-start | bytes 1048576 | tf_op jit(solution)/shard_map/all_to_all | solution.py:60
where the time goes:
time: 82 us; the launch traced here: 81.7 us
  blocking collectives  70.1 us (85%)
  local copies, waits for them, and re-layouts  5.95 us (7%)
  starting transfers between devices  3.47 us (4%)
  matrix products  1.42 us (2%)
    all_gather x1, blocking collectives, per_device(): virt_full = lax.all_gather(virt_part, ('row', 'col'), axis=0, tiled=True)  36.9 us
    all_gather x1, blocking collectives, per_device(): lax.all_gather(occ_part, ('row', 'col'), axis=0, tiled=True)  33.2 us
    all_to_all x1, starting transfers between devices, per_device(): lax.all_to_all(halfway, 'row', split_axis=0, concat_axis=2, tiled=True)  3.47 us
    unnamed x14, local copies, waits for them, and re-layouts  3.09 us
  transfers between devices with their start and end apart: 1, of which 0 were waited for; matrix products, arithmetic and copies ran while one was open for 0% of the time, Pallas kernels for 0%

commit v1 on v0

v1 whole, which is shorter than its diff:
```python
import functools

import jax
import jax.numpy as jnp
from jax import lax
from jax.experimental import pallas as pl
from jax.experimental.pallas import tpu as pltpu
from jax.sharding import PartitionSpec as P

MESH = pl.DeviceIdType.MESH
F32 = jnp.float32
BF16 = jnp.bfloat16


def loop(count, body):
    if count <= 4:
        for step in range(count):
            body(step)
    else:
        lax.fori_loop(0, count, lambda step, _: (body(step), 0)[1], 0)


def kernel(
    dims,
    pair_ref,
    occ_mask_ref,
    virt_mask_ref,
    sizes_ref,
    tensor_ref,
    occ_ref,
    virt_ref,
    out_ref,
    masked,
    packed,
    occ_all,
    virt_all,
    chosen,
    half_out,
    half_in,
    total,
    occ_send,
    occ_recv,
    pass_send,
    pass_recv,
    v1_send,
    v1_recv,
    v2_send,
    v2_recv,
    v3_send,
    v3_recv,
    h_send,
    h_recv,
):
    rows, cols, blocks, most, bs, chunk, aux = dims
    r = lax.axis_index("row")
    c = lax.axis_index("col")
    rep = lax.axis_index("rep")
    other = 1 - rep
    keep = most // 2
    wide = blocks // 2
    keep_own, keep_other = pl.ds(rep * keep, keep), pl.ds(other * keep, keep)
    wide_own, wide_other = pl.ds(rep * wide, wide), pl.ds(other * wide, wide)

    def row_at(step):
        return lax.rem(r + step, rows)

    def row_from(step):
        return lax.rem(r + rows - step, rows)

    def col_at(step):
        return lax.rem(c + step, cols)

    def col_from(step):
        return lax.rem(c + cols - step, cols)

    barrier = pltpu.get_barrier_semaphore()

    def greet(step):
        pl.semaphore_signal(
            barrier,
            inc=1,
            device_id={"row": row_at(step // cols), "col": col_at(step % cols)},
            device_id_type=MESH,
        )

    if rows * cols <= 8:
        for step in range(1, rows * cols):
            greet(step)
    else:
        lax.fori_loop(1, rows * cols, lambda step, _: (greet(step), 0)[1], 0)
    pl.semaphore_signal(barrier, inc=1, device_id={"rep": other}, device_id_type=MESH)

    def pick(column, place):
        weights, seen = [], jnp.int32(0)
        for block in range(blocks):
            here = (pair_ref[block, column] != 0).astype(jnp.int32)
            weights.append((here * (seen == place).astype(jnp.int32)).astype(F32))
            seen = seen + here
        return weights

    lane = lax.broadcasted_iota(jnp.int32, (chunk, bs), 1)
    in_block = c * chunk + lax.broadcasted_iota(jnp.int32, (chunk, bs), 0)
    row_live = (in_block < sizes_ref[r]).astype(F32)

    for block in range(blocks):
        values = occ_ref[:, block * bs : (block + 1) * bs].astype(F32)
        live = (lane < sizes_ref[block]).astype(F32)
        weight = occ_mask_ref[r, block].astype(F32)
        masked[block] = values * (live * row_live * weight)

    def pack(step):
        for j in range(keep):
            weights = pick(row_at(step), rep * keep + j)
            packed[step, j] = sum(masked[b] * weights[b] for b in range(blocks)).astype(BF16)

    loop(rows, pack)
    occ_all[r, c, keep_own] = packed[0]
    for place in range(wide):
        block = rep * wide + place
        values = virt_ref[:, pl.ds(pl.multiple_of(block * bs, bs), bs)].astype(F32)
        live = (lane < sizes_ref[block]).astype(F32)
        weight = virt_mask_ref[r, block].astype(F32)
        virt_all[c, r, block] = (values * (live * row_live * weight)).astype(BF16)

    pl.semaphore_wait(barrier, rows * cols)

    def occ_copy(step, side, source_r, source_c):
        return pltpu.make_async_remote_copy(
            src_ref=packed.at[step],
            dst_ref=occ_all.at[source_r, source_c, keep_own],
            send_sem=occ_send.at[step, side],
            recv_sem=occ_recv.at[step, side],
            device_id={"row": row_at(step), "col": col_at(side)},
            device_id_type=MESH,
        )

    def send_occ(step):
        for side in range(cols):
            if isinstance(step, int) and step == 0 and side == 0:
                continue
            occ_copy(step, side, r, c).start()

    def send_v1(step):
        v1_copy(step, r).start()

    def v1_copy(step, source_r):
        return pltpu.make_async_remote_copy(
            src_ref=virt_all.at[c, source_r, wide_own],
            dst_ref=virt_all.at[c, source_r, wide_own],
            send_sem=v1_send.at[step],
            recv_sem=v1_recv.at[step],
            device_id={"row": row_at(step)},
            device_id_type=MESH,
        )

    def v2_copy(side, source_c):
        return pltpu.make_async_remote_copy(
            src_ref=virt_all.at[source_c, :, wide_own],
            dst_ref=virt_all.at[source_c, :, wide_own],
            send_sem=v2_send.at[side],
            recv_sem=v2_recv.at[side],
            device_id={"col": col_at(side)},
            device_id_type=MESH,
        )

    def v3_copy(part):
        return pltpu.make_async_remote_copy(
            src_ref=virt_all.at[:, :, part],
            dst_ref=virt_all.at[:, :, part],
            send_sem=v3_send.at[0],
            recv_sem=v3_recv.at[0],
            device_id={"rep": other},
            device_id_type=MESH,
        )

    def pass_copy(block, part):
        return pltpu.make_async_remote_copy(
            src_ref=occ_all.at[block, :, part],
            dst_ref=occ_all.at[block, :, part],
            send_sem=pass_send.at[block],
            recv_sem=pass_recv.at[block],
            device_id={"rep": other},
            device_id_type=MESH,
        )

    def half_copy(step):
        return pltpu.make_async_remote_copy(
            src_ref=half_out.at[step],
            dst_ref=half_in.at[step],
            send_sem=h_send.at[step],
            recv_sem=h_recv.at[step],
            device_id={"row": row_at(step)},
            device_id_type=MESH,
        )

    far = rows - 1
    loop(far, lambda step: send_occ(step + 1))
    send_occ(0)
    loop(far, lambda step: send_v1(step + 1))

    tall = lax.broadcasted_iota(jnp.int32, (bs, bs), 0)
    across = lax.broadcasted_iota(jnp.int32, (bs, bs), 1)
    n_live = (across < sizes_ref[r]).astype(F32)
    picks = [pick(r, j) for j in range(most)]
    for p in range(aux):
        span = slice(p * bs, (p + 1) * bs)
        for j in range(most):
            terms = []
            for b in range(blocks):
                live = n_live * (tall < sizes_ref[b]).astype(F32) * picks[j][b]
                terms.append(tensor_ref[b * bs : (b + 1) * bs, span].astype(F32) * live)
            chosen[j * bs : (j + 1) * bs, span] = sum(terms).astype(BF16)

    def hand_on(step):
        source = row_from(step)
        for side in range(cols):
            if isinstance(step, int) and step == 0 and side == 0:
                continue
            occ_copy(step, side, source, col_from(side)).wait_recv()
        pass_copy(source, keep_own).start()

    loop(far, lambda step: hand_on(step + 1))
    hand_on(0)

    def first(step):
        goal = row_from(step)
        pass_copy(goal, keep_other).wait_recv()
        left = jnp.concatenate(
            [
                jnp.concatenate([occ_all[goal, side, j] for side in range(cols)], axis=0)
                for j in range(most)
            ],
            axis=1,
        )
        back = lax.rem(rows - step, rows)
        result = jnp.dot(left, chosen[...], preferred_element_type=F32).astype(BF16)
        if isinstance(step, int) and step == 0:
            half_in[0] = result
        else:
            half_out[back] = result
            half_copy(back).start()

    loop(far, lambda step: first(step + 1))
    first(0)

    loop(far, lambda step: v1_copy(step + 1, row_from(step + 1)).wait_recv())
    loop(cols - 1, lambda side: v2_copy(side + 1, c).start())
    loop(cols - 1, lambda side: v2_copy(side + 1, col_from(side + 1)).wait_recv())
    v3_copy(wide_own).start()
    v3_copy(wide_other).wait_recv()

    def second(step):
        source = row_from(step)
        right = jnp.concatenate(
            [
                jnp.concatenate([virt_all[side, source, block] for side in range(cols)], axis=0)
                for block in range(blocks)
            ],
            axis=1,
        )
        if not (isinstance(step, int) and step == 0):
            half_copy(step).wait_recv()
        for p in range(aux):
            term = jnp.dot(
                half_in[step, :, p * bs : (p + 1) * bs], right, preferred_element_type=F32
            )
            if isinstance(step, int) and step == 0:
                total[p] = term
            else:
                total[p] += term

    second(0)
    loop(far, lambda step: second(step + 1))
    span = blocks * bs
    for p in range(aux):
        out_ref[:, p * span : (p + 1) * span] = total[p].astype(BF16)

    def close_occ(step):
        for side in range(cols):
            if isinstance(step, int) and step == 0 and side == 0:
                continue
            occ_copy(step, side, r, c).wait_send()

    def close(step):
        close_occ(step + 1)
        v1_copy(step + 1, r).wait_send()
        half_copy(step + 1).wait_send()

    close_occ(0)
    loop(far, close)
    loop(rows, lambda block: pass_copy(block, keep_own).wait_send())
    loop(cols - 1, lambda side: v2_copy(side + 1, c).wait_send())
    v3_copy(wide_own).wait_send()


def per_device(rows, cols, integrals, occupied, virtual, pair_mask, occ_mask, virt_mask, sizes):
    total_ao, aux, ao_local = integrals.shape
    blocks = sizes.shape[0]
    bs = total_ao // blocks
    most = max(blocks // 2, 1)
    chunk = occupied.shape[0]
    dims = (rows, cols, blocks, most, bs, chunk, aux)
    smem = pl.BlockSpec(memory_space=pltpu.SMEM)
    vmem = pl.BlockSpec(memory_space=pltpu.VMEM)
    dma = pltpu.SemaphoreType.DMA
    result = pl.pallas_call(
        functools.partial(kernel, dims),
        out_shape=jax.ShapeDtypeStruct((bs, aux * total_ao), BF16),
        in_specs=[smem] * 4 + [vmem] * 3,
        out_specs=vmem,
        scratch_shapes=[
            pltpu.VMEM((blocks, chunk, bs), F32),
            pltpu.VMEM((rows, most // 2, chunk, bs), BF16),
            pltpu.VMEM((rows, cols, most, chunk, bs), BF16),
            pltpu.VMEM((cols, rows, blocks, chunk, bs), BF16),
            pltpu.VMEM((most * bs, aux * ao_local), BF16),
            pltpu.VMEM((rows, bs, aux * ao_local), BF16),
            pltpu.VMEM((rows, bs, aux * ao_local), BF16),
            pltpu.VMEM((aux, bs, total_ao), F32),
            dma((rows, cols)),
            dma((rows, cols)),
            dma((rows,)),
            dma((rows,)),
            dma((rows,)),
            dma((rows,)),
            dma((cols,)),
            dma((cols,)),
            dma((1,)),
            dma((1,)),
            dma((rows,)),
            dma((rows,)),
        ],
        compiler_params=pltpu.CompilerParams(
            collective_id=0, has_side_effects=True, vmem_limit_bytes=48 * 1024 * 1024
        ),
        name="contract",
    )(
        pair_mask,
        occ_mask,
        virt_mask,
        sizes,
        integrals.reshape(total_ao, aux * ao_local),
        occupied,
        virtual,
    )
    return result.reshape(bs, aux, total_ao)


def solution(mesh):
    in_specs = (
        P(None, ("grp", "col", "rep"), "row"),
        P(("grp", "row", "col"), None),
        P(("grp", "row", "col"), None),
        P(),
        P(),
        P(),
        P(),
    )
    out_specs = P("row", ("grp", "col", "rep"), None)
    return jax.shard_map(
        functools.partial(per_device, mesh.shape["row"], mesh.shape["col"]),
        mesh=mesh,
        in_specs=in_specs,
        out_specs=out_specs,
        check_vma=False,
    )
```

time: 82 us -> 29.1 us (0.35)
  blocking collectives: 70.1 us -> 0 us
  Pallas kernels: 0 us -> 26 us
  starting transfers between devices: 3.47 us -> 0 us
  local copies, waits for them, and re-layouts: 5.95 us -> 2.94 us
  matrix products: 1.42 us -> 0 us
    all_gather x2 -> x0, blocking collectives: 70.1 us -> none  [the longest x1 36.9 us: per_device(): virt_full = lax.all_gather(virt_part, ('row', 'col'), axis=0, tiled=True)]
    pallas_call x0 -> x1, Pallas kernels: none -> 26 us  [per_device(): pl.pallas_call(functools.partial(kernel, dims), out_shape=jax.ShapeDtypeS...]
    all_to_all x1 -> x0, starting transfers between devices: 3.47 us -> none  [per_device(): lax.all_to_all(halfway, 'row', split_axis=0, concat_axis=2, tiled=True)]
    dot_general x5 -> x0, matrix products: 1.42 us -> none  [the longest x1 0.49 us: per_device(): jnp.dot(lax.all_gather(occ_part, ('row', 'col'), axis=0, tiled=True), ope...]
    unnamed x14 -> x13, local copies, waits for them, and re-layouts: 3.09 us -> 1.77 us
    reshape x2 -> x1, local copies, waits for them, and re-layouts: 1.98 us -> 1.17 us  [per_device(): return result.reshape(bs, aux, total_ao)]
  transfers between devices with their start and end apart: 1 -> 0, of which waited for: 0 -> 0; matrix products, arithmetic and copies ran while one was open for 0% -> 0% of each run, Pallas kernels for 0% -> 0%
where the time goes in v1:
time: 29.1 us; the launch traced here: 29 us
  Pallas kernels  26 us (89%)
  local copies, waits for them, and re-layouts  2.94 us (10%)
    pallas_call x1, Pallas kernels, per_device(): pl.pallas_call(functools.partial(kernel, dims), out_shape=jax.ShapeDtypeS...  26 us
    unnamed x13, local copies, waits for them, and re-layouts  1.77 us
    reshape x1, local copies, waits for them, and re-layouts, per_device(): return result.reshape(bs, aux, total_ao)  1.17 us

profile of v1, /device:TPU:0, one launch (start us, length us, event | category | flops | bytes accessed | tf_op | source)
XLA Modules:
  0.0 29.0 jit_solution(17246844707730020710)
XLA Ops:
  0.0 0.0 copy-start
  0.0 0.0 copy-start.1
  0.0 0.0 copy-start.2
  0.0 0.0 copy-start.3
  0.0 0.0 copy-start.4
  0.0 1.2 %copy.10 = bf16[64,8,4,128]{3,1,2,0:T(8,128)(2,1)S(1)} copy(bf16[64,8,4,128]{3,2,1,0:T(4,128)(2,1)} %bitcast.5) | data formatting | bytes 1048576
  1.2 0.0 copy-start.5
  1.2 0.0 copy-done
  1.2 0.0 copy-done.1
  1.2 0.0 copy-done.2
  1.2 0.0 copy-done.3
  1.2 0.0 copy-done.4
  1.2 0.6 %copy-done.5 = s32[4]{0:T(128)S(1)} copy-done((s32[4]{0:T(128)S(1)}, s32[4]{0:T(128)}, u32[]{:S(2)}) %copy-start.5) | copy-done | bytes 40
  1.8 26.0 %contract.1 = bf16[128,2048]{1,0:T(8,128)(2,1)S(1)} custom-call(s32[4,4]{1,0:T(4,128)S(1)} %copy-done.2, s32[4,4]{1,0:T(4,128)S(1)} %copy-done.3, s32[4,4]{1,0:T(4,128)S(1)} %copy-done.4, s32[4]{0:T(128)S(1)} %copy-done.5, bf16[512,512]{1,0:T(8,128)(2,1)S(1)} %bitcast.4, bf16[64,512]{1,0:T(8,128)(2,1)S(1)} %copy-done, bf16[64,512]{1,0:T(8,128)(2,1)S(1)} %copy-done.1), custom_call_target="tpu_custom_call" | custom-call | tf_op jit(solution)/shard_map/contract/pallas_call | solution.py:306
  27.8 1.2 %reshape.7 = bf16[128,4,512]{2,1,0:T(4,128)(2,1)} reshape(bf16[128,2048]{1,0:T(8,128)(2,1)S(1)} %contract.1) | data formatting | bytes 1048576 | tf_op jit(solution)/shard_map/reshape | solution.py:346
Async XLA Ops:
  0.0 1.2 %copy-start = (bf16[64,512]{1,0:T(8,128)(2,1)S(1)}, bf16[64,512]{1,0:T(8,128)(2,1)}, u32[]{:S(2)}) copy-start(bf16[64,512]{1,0:T(8,128)(2,1)} %occ_ref.1) | copy-start | bytes 196612
  0.0 1.2 %copy-start.1 = (bf16[64,512]{1,0:T(8,128)(2,1)S(1)}, bf16[64,512]{1,0:T(8,128)(2,1)}, u32[]{:S(2)}) copy-start(bf16[64,512]{1,0:T(8,128)(2,1)} %virt_ref.1) | copy-start | bytes 196612
  0.0 1.2 %copy-start.2 = (s32[4,4]{1,0:T(4,128)S(1)}, s32[4,4]{1,0:T(4,128)}, u32[]{:S(2)}) copy-start(s32[4,4]{1,0:T(4,128)} %pair_ref.1) | copy-start | bytes 196
  0.0 1.2 %copy-start.3 = (s32[4,4]{1,0:T(4,128)S(1)}, s32[4,4]{1,0:T(4,128)}, u32[]{:S(2)}) copy-start(s32[4,4]{1,0:T(4,128)} %occ_mask_ref.1) | copy-start | bytes 196
  0.0 1.2 %copy-start.4 = (s32[4,4]{1,0:T(4,128)S(1)}, s32[4,4]{1,0:T(4,128)}, u32[]{:S(2)}) copy-start(s32[4,4]{1,0:T(4,128)} %virt_mask_ref.1) | copy-start | bytes 196
  1.2 0.7 %copy-start.5 = (s32[4]{0:T(128)S(1)}, s32[4]{0:T(128)}, u32[]{:S(2)}) copy-start(s32[4]{0:T(128)} %sizes_ref.1) | copy-start | bytes 52

commit v2 on v1

--- a/solution.py
+++ b/solution.py
@@ -232,7 +232,7 @@
             ],
             axis=1,
         )
-        back = lax.rem(rows - step, rows)
+        back = (rows - step) % rows
         result = jnp.dot(left, chosen[...], preferred_element_type=F32).astype(BF16)
         if isinstance(step, int) and step == 0:
             half_in[0] = result
@@ -293,6 +293,343 @@
     v3_copy(wide_own).wait_send()
 
 
+def kernel_four(
+    dims,
+    pair_hbm,
+    occ_mask_hbm,
+    virt_mask_hbm,
+    sizes_hbm,
+    tensor_hbm,
+    occ_hbm,
+    virt_hbm,
+    out_ref,
+    masked,
+    packed,
+    occ_in,
+    virt_all,
+    chosen,
+    half_out,
+    half_in,
+    total,
+    occ_send,
+    occ_recv,
+    pass_send,
+    pass_recv,
+    h_send,
+    h_recv,
+    v1_send,
+    v1_recv,
+    v2_send,
+    v2_recv,
+    v3_send,
+    v3_recv,
+    weave,
+    loaded,
+    occ_ref,
+    virt_ref,
+    pair_ref,
+    occ_mask_ref,
+    virt_mask_ref,
+    sizes_ref,
+    load_sem,
+):
+    rows, cols, blocks, most, bs, chunk, aux = dims
+    r = lax.axis_index("row")
+    c = lax.axis_index("col")
+    rep = lax.axis_index("rep")
+    other = 1 - rep
+    upper = r // 2
+    near = r + 1 - 2 * (r % 2)
+    across = 2 - upper
+    far = 3 - 3 * upper
+    outer_int = 1 - (r + upper) % 2
+    keep = most // 2
+    wide = blocks // 2
+    keep_own = pl.ds(rep * keep, keep)
+    keep_other = pl.ds(other * keep, keep)
+    wide_own = pl.ds(rep * wide, wide)
+    wide_other = pl.ds(other * wide, wide)
+    OWN, NEAR, ACROSS, FAR = range(4)
+    mine = ACROSS + outer_int
+    rows_of = (r, near, across, far)
+    names = (OWN, NEAR, ACROSS, FAR)
+    slot_there = (OWN, NEAR, mine, mine)
+
+    barrier = pltpu.get_barrier_semaphore()
+    for step in range(1, rows * cols):
+        pl.semaphore_signal(
+            barrier,
+            inc=1,
+            device_id={"row": (r + step // cols) % rows, "col": (c + step) % cols},
+            device_id_type=MESH,
+        )
+    pl.semaphore_signal(barrier, inc=1, device_id={"rep": other}, device_id_type=MESH)
+    pairs = (
+        (pair_hbm, pair_ref),
+        (occ_mask_hbm, occ_mask_ref),
+        (sizes_hbm, sizes_ref),
+        (occ_hbm, occ_ref),
+        (virt_mask_hbm, virt_mask_ref),
+        (virt_hbm, virt_ref),
+        (tensor_hbm, loaded),
+    )
+    loads = [
+        pltpu.make_async_copy(src, dst, load_sem.at[i]) for i, (src, dst) in enumerate(pairs)
+    ]
+    for load in loads:
+        load.start()
+    for load in loads[:4]:
+        load.wait()
+
+    def pick(column, place):
+        weights, seen = [], jnp.int32(0)
+        for block in range(blocks):
+            here = (pair_ref[block, column] != 0).astype(jnp.int32)
+            weights.append((here * (seen == place).astype(jnp.int32)).astype(F32))
+            seen = seen + here
+        return weights
+
+    lane = lax.broadcasted_iota(jnp.int32, (chunk, bs), 1)
+    in_block = c * chunk + lax.broadcasted_iota(jnp.int32, (chunk, bs), 0)
+    row_live = (in_block < sizes_ref[r]).astype(F32)
+    for block in range(blocks):
+        values = occ_ref[:, block * bs : (block + 1) * bs].astype(F32)
+        live = (lane < sizes_ref[block]).astype(F32)
+        weight = occ_mask_ref[r, block].astype(F32)
+        masked[block] = values * (live * row_live * weight)
+
+    def pack(goal):
+        slabs = []
+        for j in range(keep):
+            weights = pick(goal, rep * keep + j)
+            slabs.append(sum(masked[b] * weights[b] for b in range(blocks)).astype(BF16))
+        return jnp.stack(slabs)
+
+    for slot in (NEAR, ACROSS, FAR):
+        packed[slot - 1] = pack(rows_of[slot])
+    occ_in[OWN, c, keep_own] = pack(r)
+    for load in loads[4:6]:
+        load.wait()
+    for place in range(wide):
+        block = rep * wide + place
+        values = virt_ref[:, pl.ds(pl.multiple_of(block * bs, bs), bs)].astype(F32)
+        live = (lane < sizes_ref[block]).astype(F32)
+        weight = virt_mask_ref[r, block].astype(F32)
+        virt_all[c, r, block] = (values * (live * row_live * weight)).astype(BF16)
+
+    def send(src, dst, send_sem, recv_sem, **place):
+        return pltpu.make_async_remote_copy(
+            src_ref=src,
+            dst_ref=dst,
+            send_sem=send_sem,
+            recv_sem=recv_sem,
+            device_id=place,
+            device_id_type=MESH,
+        )
+
+    def occ_copy(slot, side, there):
+        column = c if side == 0 else 1 - c
+        return send(
+            occ_in.at[OWN, c, keep_own] if slot == OWN else packed.at[slot - 1],
+            occ_in.at[there, c, keep_own],
+            occ_send.at[slot, side],
+            occ_recv.at[there, side],
+            row=rows_of[slot],
+            col=column,
+        )
+
+    def pass_copy(slot, part):
+        slab = occ_in.at[slot, :, part]
+        return send(slab, slab, pass_send.at[slot], pass_recv.at[slot], rep=other)
+
+    def half_copy(slot, there):
+        return send(
+            half_out.at[slot - 1],
+            half_in.at[there],
+            h_send.at[slot],
+            h_recv.at[there],
+            row=rows_of[slot],
+        )
+
+    def virt_copy(slot, there):
+        slab = virt_all.at[c, r, wide_own]
+        return send(slab, slab, v1_send.at[slot], v1_recv.at[there], row=rows_of[slot])
+
+    def v2_copy(column):
+        slab = virt_all.at[column, :, wide_own]
+        return send(slab, slab, v2_send.at[0], v2_recv.at[0], col=1 - c)
+
+    def v3_copy(part):
+        slab = virt_all.at[:, :, part]
+        return send(slab, slab, v3_send.at[0], v3_recv.at[0], rep=other)
+
+    pl.semaphore_wait(barrier, rows * cols)
+
+    sends = [(FAR, 0), (ACROSS, 0), (FAR, 1), (ACROSS, 1), (NEAR, 0), (NEAR, 1), (OWN, 1)]
+    for slot, side in sends:
+        occ_copy(slot, side, slot_there[slot]).start()
+    virt_copy(NEAR, NEAR).start()
+    virt_copy(ACROSS, mine).start()
+    virt_copy(FAR, mine).start()
+
+    loads[6].wait()
+    span = bs * aux
+    gap = lax.broadcasted_iota(jnp.int32, (bs, span), 1) - aux * lax.broadcasted_iota(
+        jnp.int32, (bs, span), 0
+    )
+    order = jnp.concatenate([(gap == p).astype(F32).astype(BF16) for p in range(aux)], axis=0)
+    tall = lax.broadcasted_iota(jnp.int32, (span, bs), 0)
+    n_live = (lax.broadcasted_iota(jnp.int32, (span, bs), 1) < sizes_ref[r]).astype(F32)
+    lit = [
+        loaded[b * span : (b + 1) * span, :]
+        * (n_live * (tall < aux * sizes_ref[b]).astype(F32)).astype(BF16)
+        for b in range(blocks)
+    ]
+    for j in range(most):
+        weights = pick(r, j)
+        value = sum(lit[b] * weights[b].astype(BF16) for b in range(blocks))
+        turned = jnp.dot(order, value, preferred_element_type=F32).astype(BF16)
+        for p in range(aux):
+            chosen[j * bs : (j + 1) * bs, p * bs : (p + 1) * bs] = turned[p * bs : (p + 1) * bs]
+
+    for slot in (OWN, NEAR, ACROSS, FAR):
+        for side in range(cols):
+            if slot != OWN or side:
+                occ_copy(slot, side, slot).wait_recv()
+        pass_copy(slot, keep_own).start()
+    def halfway(slot):
+        pass_copy(slot, keep_other).wait_recv()
+        left = jnp.concatenate(
+            [
+                jnp.concatenate([occ_in[slot, side, j] for side in range(cols)], axis=0)
+                for j in range(most)
+            ],
+            axis=1,
+        )
+        return jnp.dot(left, chosen[...], preferred_element_type=F32).astype(BF16)
+
+    for slot in (FAR, ACROSS, NEAR):
+        half_out[slot - 1] = halfway(slot)
+        half_copy(slot, slot_there[slot]).start()
+    half_in[OWN] = halfway(OWN)
+
+    virt_copy(NEAR, NEAR).wait_recv()
+
+    mixed = aux * blocks
+    lead = span // mixed
+    parts = bs // lead
+    to = lax.broadcasted_iota(jnp.int32, (span, span), 0)
+    come = lax.broadcasted_iota(jnp.int32, (span, span), 1)
+    low = mixed.bit_length() - 1
+    weave[...] = (
+        (come == (to & (mixed - 1)) * lead + lax.shift_right_logical(to, low))
+        .astype(F32)
+        .astype(BF16)
+    )
+    virt_copy(ACROSS, ACROSS).wait_recv()
+    virt_copy(ACROSS, FAR).wait_recv()
+    v2_copy(c).start()
+    v2_copy(1 - c).wait_recv()
+    v3_copy(wide_own).start()
+    v3_copy(wide_other).wait_recv()
+
+    def second(slot):
+        source = rows_of[slot]
+        right = jnp.concatenate(
+            [
+                jnp.concatenate([virt_all[side, source, block] for side in range(cols)], axis=0)
+                for block in range(blocks)
+            ],
+            axis=1,
+        )
+        if slot != OWN:
+            half_copy(slot, slot).wait_recv()
+        for p in range(aux):
+            term = jnp.dot(
+                half_in[slot, :, p * bs : (p + 1) * bs], right, preferred_element_type=F32
+            )
+            if slot == OWN:
+                total[p] = term
+            else:
+                total[p] += term
+
+    for slot in (OWN, NEAR, ACROSS, FAR):
+        second(slot)
+    for part in range(parts):
+        piece = slice(part * lead, (part + 1) * lead)
+        value = jnp.concatenate(
+            [
+                total[p, piece, t * bs : (t + 1) * bs].astype(BF16)
+                for t in range(blocks)
+                for p in range(aux)
+            ],
+            axis=0,
+        )
+        turned = jnp.dot(weave[...], value, preferred_element_type=F32).astype(BF16)
+        out_ref[part * span : (part + 1) * span, :] = turned
+
+    for slot, side in sends:
+        occ_copy(slot, side, slot_there[slot]).wait_send()
+    for slot in names:
+        pass_copy(slot, keep_own).wait_send()
+        if slot != OWN:
+            half_copy(slot, slot_there[slot]).wait_send()
+    virt_copy(NEAR, NEAR).wait_send()
+    virt_copy(ACROSS, mine).wait_send()
+    virt_copy(FAR, mine).wait_send()
+    v2_copy(c).wait_send()
+    v3_copy(wide_own).wait_send()
+
+
+def call_four(dims, operands):
+    rows, cols, blocks, most, bs, chunk, aux = dims
+    span = aux * bs
+    vmem = pl.BlockSpec(memory_space=pltpu.VMEM)
+    dma = pltpu.SemaphoreType.DMA
+    one, slots = dma((1,)), dma((4,))
+    return pl.pallas_call(
+        functools.partial(kernel_four, dims),
+        out_shape=jax.ShapeDtypeStruct((bs * blocks * aux, bs), BF16),
+        in_specs=[pl.BlockSpec(memory_space=pl.ANY)] * 7,
+        out_specs=vmem,
+        scratch_shapes=[
+            pltpu.VMEM((blocks, chunk, bs), F32),
+            pltpu.VMEM((3, most // 2, chunk, bs), BF16),
+            pltpu.VMEM((4, cols, most, chunk, bs), BF16),
+            pltpu.VMEM((cols, rows, blocks, chunk, bs), BF16),
+            pltpu.VMEM((most * bs, span), BF16),
+            pltpu.VMEM((3, bs, span), BF16),
+            pltpu.VMEM((4, bs, span), BF16),
+            pltpu.VMEM((aux, bs, blocks * bs), F32),
+            dma((4, cols)),
+            dma((4, cols)),
+            slots,
+            slots,
+            slots,
+            slots,
+            slots,
+            slots,
+            one,
+            one,
+            one,
+            one,
+            pltpu.VMEM((span, span), BF16),
+            pltpu.VMEM((blocks * span, bs), BF16),
+            pltpu.VMEM((chunk, blocks * bs), BF16),
+            pltpu.VMEM((chunk, blocks * bs), BF16),
+            pltpu.SMEM((blocks, blocks), jnp.int32),
+            pltpu.SMEM((blocks, blocks), jnp.int32),
+            pltpu.SMEM((blocks, blocks), jnp.int32),
+            pltpu.SMEM((blocks,), jnp.int32),
+            dma((7,)),
+        ],
+        compiler_params=pltpu.CompilerParams(
+            collective_id=0, has_side_effects=True, vmem_limit_bytes=60 * 1024 * 1024
+        ),
+        name="contract",
+    )(*operands)
+
+
 def per_device(rows, cols, integrals, occupied, virtual, pair_mask, occ_mask, virt_mask, sizes):
     total_ao, aux, ao_local = integrals.shape
     blocks = sizes.shape[0]
@@ -300,6 +637,13 @@
     most = max(blocks // 2, 1)
     chunk = occupied.shape[0]
     dims = (rows, cols, blocks, most, bs, chunk, aux)
+    if rows == 4 and cols == 2 and most % 2 == 0 and blocks == rows:
+        flat = integrals.reshape(total_ao * aux, ao_local)
+        result = call_four(
+            dims, (pair_mask, occ_mask, virt_mask, sizes, flat, occupied, virtual)
+        )
+        result = result.reshape(bs, blocks, aux, bs).transpose(0, 2, 1, 3)
+        return result.reshape(bs, aux, total_ao)
     smem = pl.BlockSpec(memory_space=pltpu.SMEM)
     vmem = pl.BlockSpec(memory_space=pltpu.VMEM)
     dma = pltpu.SemaphoreType.DMA

time: 29.1 us -> 27.7 us (0.952)
  the two profiles are of different devices: /device:TPU:0 before, /device:TPU:9 now
where the time goes in v2:
time: 27.7 us; the launch traced here: 27.6 us
  Pallas kernels  25.6 us (92%)
  local copies, waits for them, and re-layouts  2.02 us (7%)
    pallas_call x1, Pallas kernels, call_four(): pl.pallas_call(functools.partial(kernel_four, dims), out_shape=jax.ShapeD...  25.6 us
    unnamed x1, local copies, waits for them, and re-layouts  2.02 us

profile of v2, /device:TPU:9, one launch (start us, length us, event | category | flops | bytes accessed | tf_op | source)
XLA Modules:
  0.0 27.6 jit_solution(13672002364759093867)
XLA Ops:
  0.0 25.6 %contract.1 = bf16[2048,128]{1,0:T(8,128)(2,1)} custom-call(s32[4,4]{1,0:T(4,128)} %pair_hbm.1, s32[4,4]{1,0:T(4,128)} %occ_mask_hbm.1, s32[4,4]{1,0:T(4,128)} %virt_mask_hbm.1, s32[4]{0:T(128)} %sizes_hbm.1, bf16[2048,128]{1,0:T(8,128)(2,1)} %bitcast.7, bf16[64,512]{1,0:T(8,128)(2,1)} %occ_hbm.1, bf16[64,512]{1,0:T(8,128)(2,1)} %virt_hbm.1), custom_call_target="tpu_custom_call" | custom-call | tf_op jit(solution)/shard_map/contract/pallas_call | solution.py:590
  25.6 2.0 %copy.10 = bf16[128,4,512]{2,1,0:T(4,128)(2,1)} copy(bf16[128,4,512]{2,1,0:T(4,128)(2,1)} %bitcast.6) | data formatting | bytes 1048576

commit v3 on v2

--- a/solution.py
+++ b/solution.py
@@ -323,7 +323,6 @@
     v2_recv,
     v3_send,
     v3_recv,
-    weave,
     loaded,
     occ_ref,
     virt_ref,
@@ -492,7 +491,7 @@
         for p in range(aux):
             chosen[j * bs : (j + 1) * bs, p * bs : (p + 1) * bs] = turned[p * bs : (p + 1) * bs]
 
-    for slot in (OWN, NEAR, ACROSS, FAR):
+    for slot in (FAR, ACROSS, NEAR, OWN):
         for side in range(cols):
             if slot != OWN or side:
                 occ_copy(slot, side, slot).wait_recv()
@@ -515,17 +514,6 @@
 
     virt_copy(NEAR, NEAR).wait_recv()
 
-    mixed = aux * blocks
-    lead = span // mixed
-    parts = bs // lead
-    to = lax.broadcasted_iota(jnp.int32, (span, span), 0)
-    come = lax.broadcasted_iota(jnp.int32, (span, span), 1)
-    low = mixed.bit_length() - 1
-    weave[...] = (
-        (come == (to & (mixed - 1)) * lead + lax.shift_right_logical(to, low))
-        .astype(F32)
-        .astype(BF16)
-    )
     virt_copy(ACROSS, ACROSS).wait_recv()
     virt_copy(ACROSS, FAR).wait_recv()
     v2_copy(c).start()
@@ -555,18 +543,8 @@
 
     for slot in (OWN, NEAR, ACROSS, FAR):
         second(slot)
-    for part in range(parts):
-        piece = slice(part * lead, (part + 1) * lead)
-        value = jnp.concatenate(
-            [
-                total[p, piece, t * bs : (t + 1) * bs].astype(BF16)
-                for t in range(blocks)
-                for p in range(aux)
-            ],
-            axis=0,
-        )
-        turned = jnp.dot(weave[...], value, preferred_element_type=F32).astype(BF16)
-        out_ref[part * span : (part + 1) * span, :] = turned
+    for p in range(aux):
+        out_ref[p] = total[p].astype(BF16)
 
     for slot, side in sends:
         occ_copy(slot, side, slot_there[slot]).wait_send()
@@ -581,6 +559,43 @@
     v3_copy(wide_own).wait_send()
 
 
+def weave_kernel(aux, tiles, bs, lead, in_ref, out_ref):
+    mixed = aux * tiles
+    span = mixed * lead
+    to = lax.broadcasted_iota(jnp.int32, (span, span), 0)
+    come = lax.broadcasted_iota(jnp.int32, (span, span), 1)
+    low = mixed.bit_length() - 1
+    weave = (
+        (come == (to & (mixed - 1)) * lead + lax.shift_right_logical(to, low))
+        .astype(F32)
+        .astype(BF16)
+    )
+    for part in range(in_ref.shape[1] // lead):
+        piece = slice(part * lead, (part + 1) * lead)
+        value = jnp.concatenate(
+            [in_ref[p, piece, t * bs : (t + 1) * bs] for t in range(tiles) for p in range(aux)],
+            axis=0,
+        )
+        out_ref[part * span : (part + 1) * span, :] = jnp.dot(
+            weave, value, preferred_element_type=F32
+        ).astype(BF16)
+
+
+def call_weave(value):
+    aux, bs, wide = value.shape
+    tiles = wide // bs
+    steps = 2
+    return pl.pallas_call(
+        functools.partial(weave_kernel, aux, tiles, bs, 16),
+        grid=(steps,),
+        out_shape=jax.ShapeDtypeStruct((bs * tiles * aux, bs), BF16),
+        in_specs=[pl.BlockSpec((aux, bs // steps, wide), lambda i: (0, i, 0))],
+        out_specs=pl.BlockSpec((bs * tiles * aux // steps, bs), lambda i: (i, 0)),
+        compiler_params=pltpu.CompilerParams(vmem_limit_bytes=60 * 1024 * 1024),
+        name="weave",
+    )(value)
+
+
 def call_four(dims, operands):
     rows, cols, blocks, most, bs, chunk, aux = dims
     span = aux * bs
@@ -589,7 +604,7 @@
     one, slots = dma((1,)), dma((4,))
     return pl.pallas_call(
         functools.partial(kernel_four, dims),
-        out_shape=jax.ShapeDtypeStruct((bs * blocks * aux, bs), BF16),
+        out_shape=jax.ShapeDtypeStruct((aux, bs, blocks * bs), BF16),
         in_specs=[pl.BlockSpec(memory_space=pl.ANY)] * 7,
         out_specs=vmem,
         scratch_shapes=[
@@ -613,7 +628,6 @@
             one,
             one,
             one,
-            pltpu.VMEM((span, span), BF16),
             pltpu.VMEM((blocks * span, bs), BF16),
             pltpu.VMEM((chunk, blocks * bs), BF16),
             pltpu.VMEM((chunk, blocks * bs), BF16),
@@ -642,7 +656,7 @@
         result = call_four(
             dims, (pair_mask, occ_mask, virt_mask, sizes, flat, occupied, virtual)
         )
-        result = result.reshape(bs, blocks, aux, bs).transpose(0, 2, 1, 3)
+        result = call_weave(result).reshape(bs, blocks, aux, bs).transpose(0, 2, 1, 3)
         return result.reshape(bs, aux, total_ao)
     smem = pl.BlockSpec(memory_space=pltpu.SMEM)
     vmem = pl.BlockSpec(memory_space=pltpu.VMEM)

time: 27.7 us -> 27.1 us (0.978)
  the two profiles are of different devices: /device:TPU:9 before, /device:TPU:0 now
where the time goes in v3:
time: 27.1 us; the launch traced here: 26.8 us
  Pallas kernels  26.8 us (99%)
    pallas_call x1, Pallas kernels, call_four(): pl.pallas_call(functools.partial(kernel_four, dims), out_shape=jax.ShapeD...  24.5 us
    pallas_call x1, Pallas kernels, call_weave(): pl.pallas_call(functools.partial(weave_kernel, aux, tiles, bs, 16), grid=...  2.26 us

profile of v3, /device:TPU:0, one launch (start us, length us, event | category | flops | bytes accessed | tf_op | source)
XLA Modules:
  0.0 26.8 jit_solution(12938046264949406374)
XLA Ops:
  0.0 24.5 %contract.1.in_ref = bf16[4,128,512]{2,1,0:T(8,128)(2,1)} custom-call(s32[4,4]{1,0:T(4,128)} %pair_hbm.1, s32[4,4]{1,0:T(4,128)} %occ_mask_hbm.1, s32[4,4]{1,0:T(4,128)} %virt_mask_hbm.1, s32[4]{0:T(128)} %sizes_hbm.1, bf16[2048,128]{1,0:T(8,128)(2,1)} %bitcast.6, bf16[64,512]{1,0:T(8,128)(2,1)} %occ_hbm.1, bf16[64,512]{1,0:T(8,128)(2,1)} %virt_hbm.1), custom_call_target="tpu_custom_call" | custom-call | tf_op jit(solution)/shard_map/contract/pallas_call | solution.py:605
  24.5 2.3 %weave.1 = bf16[2048,128]{1,0:T(8,128)(2,1)} custom-call(bf16[4,128,512]{2,1,0:T(8,128)(2,1)} %contract.1.in_ref), custom_call_target="tpu_custom_call" | custom-call | tf_op jit(solution)/shard_map/weave/pallas_call | solution.py:588

commit v4 on v3

--- a/solution.py
+++ b/solution.py
@@ -407,15 +407,6 @@
     for slot in (NEAR, ACROSS, FAR):
         packed[slot - 1] = pack(rows_of[slot])
     occ_in[OWN, c, keep_own] = pack(r)
-    for load in loads[4:6]:
-        load.wait()
-    for place in range(wide):
-        block = rep * wide + place
-        values = virt_ref[:, pl.ds(pl.multiple_of(block * bs, bs), bs)].astype(F32)
-        live = (lane < sizes_ref[block]).astype(F32)
-        weight = virt_mask_ref[r, block].astype(F32)
-        virt_all[c, r, block] = (values * (live * row_live * weight)).astype(BF16)
-
     def send(src, dst, send_sem, recv_sem, **place):
         return pltpu.make_async_remote_copy(
             src_ref=src,
@@ -454,19 +445,27 @@
         slab = virt_all.at[c, r, wide_own]
         return send(slab, slab, v1_send.at[slot], v1_recv.at[there], row=rows_of[slot])
 
-    def v2_copy(column):
-        slab = virt_all.at[column, :, wide_own]
-        return send(slab, slab, v2_send.at[0], v2_recv.at[0], col=1 - c)
-
-    def v3_copy(part):
-        slab = virt_all.at[:, :, part]
-        return send(slab, slab, v3_send.at[0], v3_recv.at[0], rep=other)
+    def v2_copy(slot, column):
+        slab = virt_all.at[column, rows_of[slot], wide_own]
+        return send(slab, slab, v2_send.at[slot], v2_recv.at[slot], col=1 - c)
+
+    def v3_copy(slot, part):
+        slab = virt_all.at[:, rows_of[slot], part]
+        return send(slab, slab, v3_send.at[slot], v3_recv.at[slot], rep=other)
 
     pl.semaphore_wait(barrier, rows * cols)
 
     sends = [(FAR, 0), (ACROSS, 0), (FAR, 1), (ACROSS, 1), (NEAR, 0), (NEAR, 1), (OWN, 1)]
     for slot, side in sends:
         occ_copy(slot, side, slot_there[slot]).start()
+    for load in loads[4:6]:
+        load.wait()
+    for place in range(wide):
+        block = rep * wide + place
+        values = virt_ref[:, pl.ds(pl.multiple_of(block * bs, bs), bs)].astype(F32)
+        live = (lane < sizes_ref[block]).astype(F32)
+        weight = virt_mask_ref[r, block].astype(F32)
+        virt_all[c, r, block] = (values * (live * row_live * weight)).astype(BF16)
     virt_copy(NEAR, NEAR).start()
     virt_copy(ACROSS, mine).start()
     virt_copy(FAR, mine).start()
@@ -512,17 +511,17 @@
         half_copy(slot, slot_there[slot]).start()
     half_in[OWN] = halfway(OWN)
 
-    virt_copy(NEAR, NEAR).wait_recv()
-
-    virt_copy(ACROSS, ACROSS).wait_recv()
-    virt_copy(ACROSS, FAR).wait_recv()
-    v2_copy(c).start()
-    v2_copy(1 - c).wait_recv()
-    v3_copy(wide_own).start()
-    v3_copy(wide_other).wait_recv()
+    v2_copy(OWN, c).start()
+    for slot in (NEAR, ACROSS, FAR):
+        virt_copy(slot, slot).wait_recv()
+        v2_copy(slot, c).start()
+    for slot in names:
+        v2_copy(slot, 1 - c).wait_recv()
+        v3_copy(slot, wide_own).start()
 
     def second(slot):
         source = rows_of[slot]
+        v3_copy(slot, wide_other).wait_recv()
         right = jnp.concatenate(
             [
                 jnp.concatenate([virt_all[side, source, block] for side in range(cols)], axis=0)
@@ -555,8 +554,9 @@
     virt_copy(NEAR, NEAR).wait_send()
     virt_copy(ACROSS, mine).wait_send()
     virt_copy(FAR, mine).wait_send()
-    v2_copy(c).wait_send()
-    v3_copy(wide_own).wait_send()
+    for slot in names:
+        v2_copy(slot, c).wait_send()
+        v3_copy(slot, wide_own).wait_send()
 
 
 def weave_kernel(aux, tiles, bs, lead, in_ref, out_ref):
@@ -584,7 +584,7 @@
 def call_weave(value):
     aux, bs, wide = value.shape
     tiles = wide // bs
-    steps = 2
+    steps = 1
     return pl.pallas_call(
         functools.partial(weave_kernel, aux, tiles, bs, 16),
         grid=(steps,),
@@ -601,7 +601,7 @@
     span = aux * bs
     vmem = pl.BlockSpec(memory_space=pltpu.VMEM)
     dma = pltpu.SemaphoreType.DMA
-    one, slots = dma((1,)), dma((4,))
+    slots = dma((4,))
     return pl.pallas_call(
         functools.partial(kernel_four, dims),
         out_shape=jax.ShapeDtypeStruct((aux, bs, blocks * bs), BF16),
@@ -624,10 +624,10 @@
             slots,
             slots,
             slots,
-            one,
-            one,
-            one,
-            one,
+            slots,
+            slots,
+            slots,
+            slots,
             pltpu.VMEM((blocks * span, bs), BF16),
             pltpu.VMEM((chunk, blocks * bs), BF16),
             pltpu.VMEM((chunk, blocks * bs), BF16),

time: 27.1 us -> 27.2 us (level)
  no operation moved by 1% of the time
where the time goes in v4:
time: 27.2 us; the launch traced here: 26.9 us
  Pallas kernels  26.9 us (99%)
    pallas_call x1, Pallas kernels, call_four(): pl.pallas_call(functools.partial(kernel_four, dims), out_shape=jax.ShapeD...  24.7 us
    pallas_call x1, Pallas kernels, call_weave(): pl.pallas_call(functools.partial(weave_kernel, aux, tiles, bs, 16), grid=...  2.26 us

profile of v4, /device:TPU:0, one launch (start us, length us, event | category | flops | bytes accessed | tf_op | source)
XLA Modules:
  0.0 26.9 jit_solution(646166387287728582)
XLA Ops:
  0.0 24.7 %contract.1.in_ref = bf16[4,128,512]{2,1,0:T(8,128)(2,1)} custom-call(s32[4,4]{1,0:T(4,128)} %pair_hbm.1, s32[4,4]{1,0:T(4,128)} %occ_mask_hbm.1, s32[4,4]{1,0:T(4,128)} %virt_mask_hbm.1, s32[4]{0:T(128)} %sizes_hbm.1, bf16[2048,128]{1,0:T(8,128)(2,1)} %bitcast.6, bf16[64,512]{1,0:T(8,128)(2,1)} %occ_hbm.1, bf16[64,512]{1,0:T(8,128)(2,1)} %virt_hbm.1), custom_call_target="tpu_custom_call" | custom-call | tf_op jit(solution)/shard_map/contract/pallas_call | solution.py:605
  24.7 2.3 %weave.1 = bf16[2048,128]{1,0:T(8,128)(2,1)} custom-call(bf16[4,128,512]{2,1,0:T(8,128)(2,1)} %contract.1.in_ref), custom_call_target="tpu_custom_call" | custom-call | tf_op jit(solution)/shard_map/weave/pallas_call | solution.py:588
